TPU v7x, 32 devices: a whole 2x2x4 slice. The times are simulated.
32 devices in a mesh: dp: 2 (over x), seq: 2 (over y), tensor: 8 (over z, core).
Axes of the slice: x: 2, y: 2, z: 4, core: 2. Of those that a mesh axis runs over, the one named last changes fastest.
Arguments:
- activations: bfloat16 [4, 384, 28672], P('dp', 'seq', 'tensor'), may hold values from -6 to 6
- gradients: bfloat16 [4, 384, 8192], P('dp', 'seq', 'tensor'), may hold values from -6 to 6
- basis_in: bfloat16 [28672, 128], P('tensor', 'seq'), may hold values from -0.03125 to 0.03125
- basis_out: bfloat16 [8192, 768], P('tensor', 'seq'), may hold values from -0.0625 to 0.0625
Outputs:
- corrected: float32 [128, 768], P(('seq', 'tensor'))
All inputs are finite; a program needn't handle non-finite values.
Results may differ from a plain program's by a relative error of at most 0.0034.
Values may be sent and summed in bfloat16 or wider, within the bound.
A program may use at most 64 MiB of HBM per device.

v0:
```python
import jax
import jax.numpy as jnp
from jax import lax
from jax.sharding import PartitionSpec as P


def body(activations, gradients, basis_in, basis_out):
    seq_count = lax.axis_size("seq")
    tensor_count = lax.axis_size("tensor")
    replica_count = lax.axis_size("dp")
    seqs_local = activations.shape[0]
    len_local = activations.shape[1]
    width_local = activations.shape[2]
    grad_partial = jnp.einsum(
        "sci,ij->scj",
        gradients,
        lax.all_gather(basis_out, "seq", axis=1, tiled=True),
        preferred_element_type=jnp.float32,
    )
    projected_grad = lax.psum(grad_partial, "tensor").astype(jnp.bfloat16)
    whole_basis = lax.all_gather(basis_in, "seq", axis=1, tiled=True)
    col_total = whole_basis.shape[1]
    per_device = col_total // (seq_count * tensor_count)
    arranged = whole_basis.reshape(width_local, seq_count, tensor_count, per_device)
    group_rows = seq_count * per_device
    product = jnp.einsum(
        "isTj,qci->Tsjqc", arranged, activations, preferred_element_type=jnp.float32
    )
    flat_act = lax.psum_scatter(
        product.reshape(group_rows * lax.axis_size("tensor"), seqs_local * len_local),
        "tensor",
        scatter_dimension=0,
        tiled=True,
    ).astype(jnp.bfloat16)
    projected_act = flat_act.reshape(flat_act.shape[0], seqs_local, len_local)
    partial_blocks = jnp.einsum(
        "rqc,qcj->qrj", projected_act, projected_grad, preferred_element_type=jnp.float32
    )
    blocks = lax.psum_scatter(partial_blocks, "seq", scatter_dimension=1, tiled=True)
    squared = jnp.sum(blocks * blocks, axis=0)
    summed = lax.psum(squared, "dp")
    return summed / (seqs_local * replica_count * len_local * seq_count)


def solution(mesh):
    return jax.shard_map(
        body,
        mesh=mesh,
        in_specs=(
            P("dp", "seq", "tensor"),
            P("dp", "seq", "tensor"),
            P("tensor", "seq"),
            P("tensor", "seq"),
        ),
        out_specs=P(("seq", "tensor"), None),
        check_vma=False,
    )
```

profile of v0, /device:TPU:0, one launch (start us, length us, event | category | flops | bytes accessed | tf_op | source)
XLA Modules:
  0.0 146.3 jit_solution(6064606000209783630)
XLA Ops:
  7.4 0.0 copy-start
  7.4 0.0 reduce-scatter.3.cloned.1.call-start
  7.4 14.5 %all_gather.6 = bf16[3584,128]{0,1:T(8,128)(2,1)S(1)} all-gather(bf16[3584,64]{0,1:T(8,128)(2,1)} %param.6), channel_id=1, replica_groups=mesh['dp'=2,'seq'=2,'tensor'=8] {'seq'}, dimensions={1}, use_global_device_ids=true | all-gather | bytes 1376256 | tf_op jit(solution)/shard_map/all_gather | solution.py:21
  21.9 0.0 copy-done
  21.9 1.0 fusion.4
  22.9 0.2 copy.5
  23.1 0.9 reshape.10
  24.0 0.0 reduce-scatter.3.cloned.1.call-update
  24.0 0.0 all-gather.2.cloned.1.call-start
  24.1 0.5 all-gather.2.cloned.1.call-update
  24.6 0.0 reduce-scatter.5.cloned.1.call-start
  24.7 31.2 %reduce-scatter.3.cloned.1.call-done = f32[16,384]{1,0:T(8,128)} async-done(((f32[128,384]{1,0:T(8,128)}), f32[16,384]{1,0:T(8,128)}) %reduce-scatter.3.cloned.1.call-update) | async-done | bytes 24592 | tf_op jit(solution)/shard_map/reduce_scatter | solution.py:29
  55.9 0.7 convert_element_type.6
  56.6 0.1 reshape.11
  56.7 0.0 all-gather.2.cloned.1.call-done
  56.7 3.4 %fusion.2 = f32[2,192,768]{2,1,0:T(8,128)} fusion(bf16[2,192,1024]{2,1,0:T(8,128)(2,1)} %param.5, bf16[1024,768]{1,0:T(8,128)(2,1)} %all-gather.2.cloned.1.call-done), kind=kOutput, calls=%fused_computation.2 | convolution fusion | flops 603979776 | bytes 3538944 | tf_op jit(solution)/shard_map/sci,ij->scj/dot_general | solution.py:14
  60.2 57.5 %all-reduce.1 = bf16[2,192,768]{2,1,0:T(8,128)(2,1)S(1)} all-reduce(f32[2,192,768]{2,1,0:T(8,128)} %fusion.2), channel_id=1, replica_groups=mesh['dp'=2,'seq'=2,'tensor'=8] {'tensor'}, use_global_device_ids=true, to_apply=%region_1.0 | all-reduce | flops 294912 | bytes 1769472 | tf_op jit(solution)/shard_map/psum | solution.py:20
  117.7 0.8 fusion.7
  118.5 0.0 reduce-scatter.5.cloned.1.call-update
  118.5 10.6 %reduce-scatter.5.cloned.1.call-done = f32[2,8,768]{2,1,0:T(8,128)} async-done(((f32[2,16,768]{2,1,0:T(8,128)}), f32[2,8,768]{2,1,0:T(8,128)}) %reduce-scatter.5.cloned.1.call-update) | async-done | bytes 49168 | tf_op jit(solution)/shard_map/reduce_scatter | solution.py:39
  129.2 0.8 multiply_reduce_fusion
  130.0 8.3 %psum.15 = f32[8,768]{1,0:T(8,128)S(1)} all-reduce(f32[8,768]{1,0:T(8,128)S(1)} %multiply_reduce_fusion), channel_id=1, replica_groups=mesh['dp'=2,'seq'=2,'tensor'=8] {'dp'}, use_global_device_ids=true, to_apply=%region_4.0 | all-reduce | flops 6144 | bytes 49152 | tf_op jit(solution)/shard_map/psum | solution.py:41
  138.3 0.6 broadcast_multiply_fusion
Async XLA Ops:
  7.4 14.5 %copy-start = (bf16[2,192,3584]{2,1,0:T(8,128)(2,1)S(1)}, bf16[2,192,3584]{2,1,0:T(8,128)(2,1)}, u32[]{:S(2)}) copy-start(bf16[2,192,3584]{2,1,0:T(8,128)(2,1)} %param.4) | copy-start | bytes 8257540
  7.4 48.5 %reduce-scatter.3.cloned.1.call-start = ((), (), s32[]{:S(2)}) async-start(), calls=%async_computation.2 | async-start | bytes 221184 | tf_op jit(solution)/shard_map/reduce_scatter | solution.py:29
  24.0 32.7 %all-gather.2.cloned.1.call-start = ((), (), s32[]{:S(2)}) async-start(), calls=%async_computation.3 | async-start | bytes 2359296 | tf_op jit(solution)/shard_map/all_gather | solution.py:17
  24.6 104.6 %reduce-scatter.5.cloned.1.call-start = ((), (), s32[]{:S(2)}) async-start(), calls=%async_computation.4 | async-start | bytes 147456 | tf_op jit(solution)/shard_map/reduce_scatter | solution.py:39
Sparse Core Ops, SparseCore 0:
  24.1 31.7 reduce-scatter.2
Sparse Core Ops, SparseCore 1:
  26.0 28.5 all-gather.1
  118.6 10.5 reduce-scatter.4
where the time goes:
time: 147 us; the launch traced here: 146 us
  blocking collectives  80.3 us (55%)
  waiting for transfers between devices  42.4 us (29%)
  between operations  14.9 us (10%)
  matrix products  5.3 us (4%)
  other arithmetic  2.16 us (1%)
    psum x1, blocking collectives, body(): projected_grad = lax.psum(grad_partial, 'tensor').astype(jnp.bfloat16)  57.5 us
    reduce_scatter x1, waiting for transfers between devices, body(): lax.psum_scatter(product.reshape(group_rows * lax.axis_size('tensor'), se...  31.2 us
    all_gather x1, blocking collectives, body(): whole_basis = lax.all_gather(basis_in, 'seq', axis=1, tiled=True)  14.5 us
    reduce_scatter x1, waiting for transfers between devices, body(): lax.psum_scatter(partial_blocks, 'seq', scatter_dimension=1, tiled=True)  10.6 us
    psum x1, blocking collectives, body(): summed = lax.psum(squared, 'dp')  8.3 us
    dot_general x1, matrix products, body(): jnp.einsum('sci,ij->scj', gradients, lax.all_gather(basis_out, 'seq', axi...  3.45 us
  transfers between devices with their start and end apart: 3, of which 2 were waited for; matrix products, arithmetic and copies ran while one was open for 1% of the time, Pallas kernels for 0%

commit v1 on v0

--- a/solution.py
+++ b/solution.py
@@ -1,10 +1,284 @@
+import functools
+
 import jax
 import jax.numpy as jnp
 from jax import lax
+from jax.experimental import pallas as pl
+from jax.experimental.pallas import tpu as pltpu
 from jax.sharding import PartitionSpec as P
 
-
-def body(activations, gradients, basis_in, basis_out):
+MESH = pl.DeviceIdType.MESH
+F32 = jnp.float32
+BF16 = jnp.bfloat16
+CHUNKS = 2
+
+
+def kernel(
+    dims,
+    act_hbm, grad_hbm, pin_hbm, bout_hbm, out_ref,
+    act, grad, pin_own, pin_oth, bout_own, bout_oth,
+    gpart, gmate, gown, gsend, grecv,
+    apart, arecv, afull,
+    bpart, brecv, spad, strans, frecv,
+    local_sem, ysend, yrecv, xsend, xrecv, msend, mrecv, zsend, zrecv,
+    a1send, a1recv, a2send, a2recv, bsend, brecv_sem, fsend, frecv_sem,
+):
+    dps, seqs, tensors, nz, cols, count = dims
+    dp = lax.axis_index("dp")
+    y = lax.axis_index("seq")
+    t = lax.axis_index("tensor")
+    z = t // 2
+    c = lax.rem(t, 2)
+    oy = 1 - y
+    odp = 1 - dp
+    mate = z * 2 + (1 - c)
+    tokens = grad.shape[0]
+    per_seq = tokens // 2
+
+    def remote(src, dst, s, r, to):
+        copy = pltpu.make_async_remote_copy(
+            src_ref=src, dst_ref=dst, send_sem=s, recv_sem=r,
+            device_id=to, device_id_type=MESH,
+        )
+        copy.start()
+        return copy
+
+    loads = []
+    for n, (src, dst) in enumerate(
+        ((bout_hbm, bout_own), (grad_hbm, grad), (pin_hbm, pin_own), (act_hbm, act))
+    ):
+        copy = pltpu.make_async_copy(src, dst, local_sem.at[n])
+        copy.start()
+        loads.append(copy)
+
+    barrier = pltpu.get_barrier_semaphore()
+    for ddp in range(dps):
+        for d in range(tensors):
+            if ddp + d == 0:
+                continue
+            pl.semaphore_signal(
+                barrier, inc=1,
+                device_id=(lax.rem(dp + ddp, dps), y, lax.rem(t + d, tensors)),
+                device_id_type=MESH,
+            )
+    pl.semaphore_signal(barrier, inc=1, device_id=(dp, oy, t), device_id_type=MESH)
+    pl.semaphore_wait(barrier, dps * tensors)
+
+    def rows(ref, half, chunk):
+        size = ref.shape[0] // (2 * CHUNKS)
+        return pl.ds(pl.multiple_of((half * CHUNKS + chunk) * size, size), size)
+
+    sends = []
+    ycopies = []
+    for n, (src, dst) in enumerate(((pin_hbm, pin_oth), (bout_hbm, bout_oth))):
+        for k in range(CHUNKS):
+            i = n * CHUNKS + k
+            part = rows(dst, dp, k)
+            ycopies.append(
+                remote(src.at[part], dst.at[part], ysend.at[i], yrecv.at[i], (dp, oy, t))
+            )
+    sends += ycopies
+    xcopies = []
+
+    def forward(n, dst):
+        for k in range(CHUNKS):
+            i = n * CHUNKS + k
+            ycopies[i].wait_recv()
+            part = rows(dst, dp, k)
+            xcopies.append(
+                remote(dst.at[part], dst.at[part], xsend.at[i], xrecv.at[i], (odp, y, t))
+            )
+
+    def project_grad(basis, h, slot):
+        total = lax.dot_general(
+            basis[...], grad[...], (((0,), (1,)), ((), ())), preferred_element_type=F32
+        )
+        gpart[slot] = total.reshape(2, nz, cols, tokens)
+        return remote(
+            gpart.at[slot, 1 - c], gmate.at[h], msend.at[slot], mrecv.at[slot],
+            (dp, y, mate),
+        )
+
+    def scatter_grad(copy, h, slot):
+        copy.wait_recv()
+        pair = gpart[slot, c] + gmate[h]
+        gsend[slot] = pair.astype(BF16)
+        gown[slot] = gpart[slot, c, z] + gmate[h, z]
+        copies = []
+        for d in range(1, nz):
+            oz = lax.rem(z + d, nz)
+            i = slot * (nz - 1) + d - 1
+            copies.append(
+                remote(
+                    gsend.at[slot, oz], grecv.at[slot, d - 1], zsend.at[i], zrecv.at[i],
+                    (dp, y, oz * 2 + c),
+                )
+            )
+        return copies
+
+    loads[0].wait()
+    loads[1].wait()
+    mate0 = project_grad(bout_own, 0, 0)
+    forward(0, pin_oth)
+    loads[2].wait()
+    loads[3].wait()
+    half = pin_own.shape[0]
+    left_own = jnp.dot(act[:, :half], pin_own[...], preferred_element_type=F32)
+    right_own = jnp.dot(act[:, half:], pin_own[...], preferred_element_type=F32)
+    z0 = scatter_grad(mate0, 0, 0)
+
+    for k in range(CHUNKS):
+        xcopies[k].wait_recv()
+    left_oth = jnp.dot(act[:, :half], pin_oth[...], preferred_element_type=F32)
+    right_oth = jnp.dot(act[:, half:], pin_oth[...], preferred_element_type=F32)
+    kk = pin_own.shape[1]
+    lane = lax.broadcasted_iota(jnp.int32, (tokens, kk), 1)
+    low = lane < kk // 2
+    own = jnp.where(low, left_own, 0.0) + pltpu.roll(jnp.where(low, 0.0, right_own), kk // 2, 1)
+    oth = jnp.where(low, left_oth, 0.0) + pltpu.roll(jnp.where(low, 0.0, right_oth), kk // 2, 1)
+    first = jnp.where(y == 0, own, oth)
+    second = jnp.where(y == 0, oth, own)
+    apart[...] = (first + pltpu.roll(second, kk // 2, 1)).reshape(apart.shape)
+    a1 = []
+    for d in range(1, tensors):
+        ot = lax.rem(t + d, tensors)
+        a1.append(
+            remote(apart.at[ot], arecv.at[d - 1], a1send.at[d - 1], a1recv.at[d - 1], (dp, y, ot))
+        )
+
+    forward(1, bout_oth)
+    total = apart[t]
+    for d in range(1, tensors):
+        a1[d - 1].wait_recv()
+        total = total + arecv[d - 1]
+    afull[t] = total.astype(BF16)
+    a2 = []
+    for d in range(1, tensors):
+        ot = lax.rem(t + d, tensors)
+        a2.append(
+            remote(afull.at[t], afull.at[t], a2send.at[d - 1], a2recv.at[d - 1], (dp, y, ot))
+        )
+
+    for k in range(CHUNKS):
+        xcopies[CHUNKS + k].wait_recv()
+    mate1 = project_grad(bout_oth, 1, 1)
+    for copy in a2:
+        copy.wait_recv()
+    whole = afull[...].astype(F32).reshape(tokens, kk)
+    turned = pltpu.roll(whole, kk // 2, 1)
+    row = lax.broadcasted_iota(jnp.int32, (tokens, kk), 0)
+    mine = (row < per_seq) == low
+    masked0 = jnp.where(mine, jnp.where(low, whole, turned), 0.0).astype(BF16)
+    masked1 = jnp.where(mine, jnp.where(low, turned, whole), 0.0).astype(BF16)
+    z1 = scatter_grad(mate1, 1, 1)
+
+    def finish_grad(slot, copies):
+        total = gown[slot]
+        for d in range(1, nz):
+            copies[d - 1].wait_recv()
+            total = total + grecv[slot, d - 1].astype(F32)
+        return total.astype(BF16)
+
+    def outer(part, slot):
+        at = jnp.where(y == slot, 0, 1)
+        bpart[0, at] = jnp.dot(part, masked0, preferred_element_type=F32)
+        bpart[1, at] = jnp.dot(part, masked1, preferred_element_type=F32)
+
+    outer(finish_grad(0, z0), 0)
+    outer(finish_grad(1, z1), 1)
+    bcopy = remote(bpart.at[oy], brecv, bsend.at[0], brecv_sem.at[0], (dp, oy, t))
+    spad[...] = jnp.zeros_like(spad)
+    bcopy.wait_recv()
+    both = (bpart[y] + brecv[...]).reshape(2 * cols, kk)
+    square = both * both
+    spad[pl.ds(0, 2 * cols), :] = square + pltpu.roll(square, kk // 2, 1)
+    strans[...] = spad[...].T.reshape(strans.shape)
+    place = c * nz + z
+    frecv[0, place] = strans[t]
+    fcopies = []
+    for ddp in range(dps):
+        for d in range(tensors):
+            if ddp + d == 0:
+                continue
+            i = ddp * tensors + d - 1
+            ot = lax.rem(t + d, tensors)
+            fcopies.append(
+                remote(
+                    strans.at[ot], frecv.at[ddp, place], fsend.at[i], frecv_sem.at[i],
+                    (lax.rem(dp + ddp, dps), y, ot),
+                )
+            )
+    for copy in fcopies:
+        copy.wait_recv()
+    out_ref[...] = (frecv[0] + frecv[1]) / count
+    for copy in sends + xcopies + [mate0, mate1] + z0 + z1 + a1 + a2 + [bcopy] + fcopies:
+        copy.wait_send()
+
+
+def fused(activations, gradients, basis_in, basis_out):
+    dps, seqs, tensors = lax.axis_size("dp"), lax.axis_size("seq"), lax.axis_size("tensor")
+    s, length, width = activations.shape
+    gwidth = gradients.shape[2]
+    tokens = s * length
+    nz = tensors // 2
+    khalf = basis_in.shape[1]
+    jhalf = basis_out.shape[1]
+    kk = 2 * khalf
+    cols = jhalf // tensors
+    per = khalf // tensors
+    count = s * dps * length * seqs
+    packed = jnp.concatenate([basis_in[: width // 2], basis_in[width // 2 :]], axis=1)
+    dma = pltpu.SemaphoreType.DMA
+    tok_own = tokens // tensors
+    out = pl.pallas_call(
+        functools.partial(kernel, (dps, seqs, tensors, nz, cols, count)),
+        out_shape=jax.ShapeDtypeStruct((tensors, per, 128), F32),
+        in_specs=[pl.BlockSpec(memory_space=pl.ANY)] * 4,
+        out_specs=pl.BlockSpec(memory_space=pltpu.VMEM),
+        scratch_shapes=[
+            pltpu.VMEM((tokens, width), BF16),
+            pltpu.VMEM((tokens, gwidth), BF16),
+            pltpu.VMEM((width // 2, kk), BF16),
+            pltpu.VMEM((width // 2, kk), BF16),
+            pltpu.VMEM((gwidth, jhalf), BF16),
+            pltpu.VMEM((gwidth, jhalf), BF16),
+            pltpu.VMEM((2, 2, nz, cols, tokens), F32),
+            pltpu.VMEM((2, nz, cols, tokens), F32),
+            pltpu.VMEM((2, cols, tokens), F32),
+            pltpu.VMEM((2, nz, cols, tokens), BF16),
+            pltpu.VMEM((2, nz - 1, cols, tokens), BF16),
+            pltpu.VMEM((tensors, tok_own, kk), F32),
+            pltpu.VMEM((tensors - 1, tok_own, kk), F32),
+            pltpu.VMEM((tensors, tok_own, kk), BF16),
+            pltpu.VMEM((2, 2, cols, kk), F32),
+            pltpu.VMEM((2, cols, kk), F32),
+            pltpu.VMEM((128, kk), F32),
+            pltpu.VMEM((kk // per, per, 128), F32),
+            pltpu.VMEM((dps, tensors, per, 128), F32),
+            dma((4,)),
+            dma((2 * CHUNKS,)), dma((2 * CHUNKS,)),
+            dma((2 * CHUNKS,)), dma((2 * CHUNKS,)),
+            dma((2,)), dma((2,)),
+            dma((2 * (nz - 1),)), dma((2 * (nz - 1),)),
+            dma((tensors - 1,)), dma((tensors - 1,)),
+            dma((tensors - 1,)), dma((tensors - 1,)),
+            dma((1,)), dma((1,)),
+            dma((dps * tensors - 1,)), dma((dps * tensors - 1,)),
+        ],
+        compiler_params=pltpu.CompilerParams(
+            collective_id=0, has_side_effects=True, vmem_limit_bytes=40 * 1024 * 1024
+        ),
+    )(
+        activations.reshape(tokens, width),
+        gradients.reshape(tokens, gwidth),
+        packed,
+        basis_out,
+    )
+    kept = out[:, :, : 2 * cols].reshape(tensors, per, 2, cols)
+    return kept.transpose(1, 2, 0, 3).reshape(per, 2 * jhalf)
+
+
+def general(activations, gradients, basis_in, basis_out):
     seq_count = lax.axis_size("seq")
     tensor_count = lax.axis_size("tensor")
     replica_count = lax.axis_size("dp")
@@ -40,6 +314,23 @@
     squared = jnp.sum(blocks * blocks, axis=0)
     summed = lax.psum(squared, "dp")
     return summed / (seqs_local * replica_count * len_local * seq_count)
+
+
+def body(activations, gradients, basis_in, basis_out):
+    dps, seqs, tensors = lax.axis_size("dp"), lax.axis_size("seq"), lax.axis_size("tensor")
+    s, length, width = activations.shape
+    tokens = s * length
+    khalf, jhalf = basis_in.shape[1], basis_out.shape[1]
+    fits = (
+        dps == 2 and seqs == 2 and s == 2 and tensors % 2 == 0
+        and khalf == 64 and khalf % (8 * tensors) == 0
+        and tokens % (16 * tensors) == 0 and tokens % 128 == 0
+        and jhalf % (16 * tensors) == 0 and 2 * jhalf // tensors <= 128
+        and width % 256 == 0 and (width // 2) % (32 * CHUNKS) == 0
+        and gradients.shape[2] % (32 * CHUNKS) == 0
+        and tokens * width * 2 <= 8 * 1024 * 1024
+    )
+    return (fused if fits else general)(activations, gradients, basis_in, basis_out)
 
 
 def solution(mesh):

time: 147 us -> 53.6 us (0.36)
  blocking collectives: 80.3 us -> 0 us
  Pallas kernels: 0 us -> 42.7 us
  waiting for transfers between devices: 42.4 us -> 0 us
  between operations: 14.9 us -> 0.06 us
  local copies, waits for them, and re-layouts: 1.18 us -> 9.15 us
  matrix products: 5.3 us -> 0 us
    psum x2 -> x0, blocking collectives: 65.8 us -> none  [the longest x1 57.5 us: body(): projected_grad = lax.psum(grad_partial, 'tensor').astype(jnp.bfloat16)]
    pallas_call x0 -> x1, Pallas kernels: none -> 42.7 us  [fused(): pl.pallas_call(functools.partial(kernel, (dps, seqs, tensors, nz, cols, c...]
    reduce_scatter x2 -> x0, waiting for transfers between devices: 41.9 us -> none  [the longest x1 31.2 us: body(): lax.psum_scatter(product.reshape(group_rows * lax.axis_size('tensor'), se...]
    all_gather x1 -> x0, blocking collectives: 14.5 us -> none  [body(): whole_basis = lax.all_gather(basis_in, 'seq', axis=1, tiled=True)]
    unnamed x2 -> x10, local copies, waits for them, and re-layouts: 0.01 us -> 5.57 us
    dot_general x3 -> x0, matrix products: 5.3 us -> none  [the longest x1 3.45 us: body(): jnp.einsum('sci,ij->scj', gradients, lax.all_gather(basis_out, 'seq', axi...]
    slice x0 -> x1, local copies, waits for them, and re-layouts: none -> 2.01 us  [fused(): basis_in[:width // 2]]
  transfers between devices with their start and end apart: 3 -> 0, of which waited for: 2 -> 0; matrix products, arithmetic and copies ran while one was open for 1% -> 0% of each run, Pallas kernels for 0% -> 0%
where the time goes in v1:
time: 53.6 us; the launch traced here: 53.3 us
  Pallas kernels  42.7 us (80%)
  local copies, waits for them, and re-layouts  9.15 us (17%)
  other arithmetic  1.41 us (3%)
    pallas_call x1, Pallas kernels, fused(): pl.pallas_call(functools.partial(kernel, (dps, seqs, tensors, nz, cols, c...  42.7 us
    unnamed x10, local copies, waits for them, and re-layouts  5.57 us
    slice x1, local copies, waits for them, and re-layouts, fused(): basis_in[:width // 2]  2.01 us
    concatenate x1, other arithmetic, fused(): jnp.concatenate([basis_in[:width // 2], basis_in[width // 2:]], axis=1)  1.41 us

profile of v1, /device:TPU:0, one launch (start us, length us, event | category | flops | bytes accessed | tf_op | source)
XLA Modules:
  0.0 53.3 jit_solution(556877192413359694)
XLA Ops:
  0.0 0.0 copy-start.1
  0.0 0.0 copy-start
  0.0 2.0 %fusion = (bf16[1792,64]{0,1:T(8,128)(2,1)}, bf16[1792,64]{0,1:T(8,128)(2,1)}) fusion(bf16[3584,64]{0,1:T(8,128)(2,1)} %param.6), kind=kLoop, calls=%fused_computation.1 | loop fusion | bytes 917504 | tf_op jit(solution)/shard_map/slice | solution.py:230
  2.0 1.9 %copy.8 = bf16[1792,64]{1,0:T(8,128)(2,1)} copy(bf16[1792,64]{0,1:T(8,128)(2,1)} %get-tuple-element.5) | data formatting | bytes 458752
  3.9 1.9 %copy.9 = bf16[1792,64]{1,0:T(8,128)(2,1)} copy(bf16[1792,64]{0,1:T(8,128)(2,1)} %get-tuple-element.6) | data formatting | bytes 458752
  5.8 1.4 %pad_maximum_fusion.pin_hbm = bf16[1792,128]{1,0:T(8,128)(2,1)S(1)} fusion(bf16[1792,64]{1,0:T(8,128)(2,1)} %copy.9, bf16[1792,64]{1,0:T(8,128)(2,1)} %copy.8), kind=kLoop, calls=%fused_computation | loop fusion | flops 917504 | bytes 917504 | tf_op jit(solution)/shard_map/concatenate | solution.py:230
  7.3 0.0 copy-done.1
  7.3 0.0 copy-done
  7.3 0.0 copy-start.2
  7.3 1.1 %copy-done.2 = bf16[1024,384]{1,0:T(8,128)(2,1)S(1)} copy-done((bf16[1024,384]{1,0:T(8,128)(2,1)S(1)}, bf16[1024,384]{1,0:T(8,128)(2,1)}, u32[]{:S(2)}) %copy-start.2) | copy-done | bytes 786456
  8.4 42.7 %shard_map.46 = f32[8,8,128]{2,1,0:T(8,128)S(1)} custom-call(bf16[384,3584]{1,0:T(8,128)(2,1)S(1)} %bitcast.6, bf16[384,1024]{1,0:T(8,128)(2,1)S(1)} %bitcast.7, bf16[1792,128]{1,0:T(8,128)(2,1)S(1)} %pad_maximum_fusion.pin_hbm, bf16[1024,384]{1,0:T(8,128)(2,1)S(1)} %copy-done.2), custom_call_target="tpu_custom_call" | custom-call | tf_op jit(solution)/shard_map/pallas_call | solution.py:233
  51.1 0.0 copy-start.3
  51.1 0.6 %copy-done.3 = f32[8,8,128]{2,1,0:T(8,128)} copy-done((f32[8,8,128]{2,1,0:T(8,128)}, f32[8,8,128]{2,1,0:T(8,128)S(1)}, u32[]{:S(2)}) %copy-start.3) | copy-done | bytes 32792
  51.7 0.9 %reshape.14 = f32[8,8,2,48]{3,2,1,0:T(2,128)S(1)} reshape(f32[8,8,96]{2,1,0:T(8,128)} %bitcast.8) | data formatting | bytes 49152 | tf_op jit(solution)/shard_map/reshape | solution.py:277
  52.6 0.7 %reshape.15 = f32[8,768]{1,0:T(8,128)} reshape(f32[8,2,8,48]{3,2,1,0:T(8,128)S(1)} %copy.7) | data formatting | bytes 49152 | tf_op jit(solution)/shard_map/reshape | solution.py:278
  (1 shorter events, 0.0 us)
Async XLA Ops:
  0.0 7.3 %copy-start.1 = (bf16[2,192,1024]{2,1,0:T(8,128)(2,1)S(1)}, bf16[2,192,1024]{2,1,0:T(8,128)(2,1)}, u32[]{:S(2)}) copy-start(bf16[2,192,1024]{2,1,0:T(8,128)(2,1)} %param.5) | copy-start | bytes 2359300
  0.0 7.3 %copy-start = (bf16[2,192,3584]{2,1,0:T(8,128)(2,1)S(1)}, bf16[2,192,3584]{2,1,0:T(8,128)(2,1)}, u32[]{:S(2)}) copy-start(bf16[2,192,3584]{2,1,0:T(8,128)(2,1)} %param.4) | copy-start | bytes 8257540
  7.3 1.1 %copy-start.2 = (bf16[1024,384]{1,0:T(8,128)(2,1)S(1)}, bf16[1024,384]{1,0:T(8,128)(2,1)}, u32[]{:S(2)}) copy-start(bf16[1024,384]{1,0:T(8,128)(2,1)} %bout_hbm.1) | copy-start | bytes 2359300
  51.1 0.6 %copy-start.3 = (f32[8,8,128]{2,1,0:T(8,128)}, f32[8,8,128]{2,1,0:T(8,128)S(1)}, u32[]{:S(2)}) copy-start(f32[8,8,128]{2,1,0:T(8,128)S(1)} %shard_map.46) | copy-start | bytes 98308

commit v2 on v1

v2 whole, which is shorter than its diff:
```python
import functools

import jax
import jax.numpy as jnp
from jax import lax
from jax.experimental import pallas as pl
from jax.experimental.pallas import tpu as pltpu
from jax.sharding import PartitionSpec as P

MESH = pl.DeviceIdType.MESH
F32 = jnp.float32
BF16 = jnp.bfloat16
CHUNKS = 2


def kernel(
    dims,
    act_hbm, grad_hbm, pin_hbm, bout_hbm, out_ref,
    act, grad, pin, bout_own, bout_oth,
    gpart, gmate, gown, gsend, grecv, gfin,
    apart, arecv, afull,
    bpart, brecv, spad, strans, frecv,
    local_sem, ysend, yrecv, xsend, xrecv, msend, mrecv, zsend, zrecv,
    a1send, a1recv, a2send, a2recv, bsend, brecv_sem, fsend, frecv_sem,
):
    dps, seqs, tensors, nz, groups, cols, count = dims
    dp = lax.axis_index("dp")
    y = lax.axis_index("seq")
    t = lax.axis_index("tensor")
    z = t // 2
    c = lax.rem(t, 2)
    oy = 1 - y
    odp = 1 - dp
    mate = z * 2 + (1 - c)
    tokens, width = act.shape
    depth = grad.shape[1]
    per_seq = tokens // 2
    kk = afull.shape[2]

    def remote(src, dst, s, r, to):
        copy = pltpu.make_async_remote_copy(
            src_ref=src, dst_ref=dst, send_sem=s, recv_sem=r,
            device_id=to, device_id_type=MESH,
        )
        copy.start()
        return copy

    loads = []
    for n, (src, dst) in enumerate(
        ((bout_hbm, bout_own), (grad_hbm, grad), (pin_hbm, pin.at[y]), (act_hbm, act))
    ):
        copy = pltpu.make_async_copy(src, dst, local_sem.at[n])
        copy.start()
        loads.append(copy)

    barrier = pltpu.get_barrier_semaphore()
    for ddp in range(dps):
        for d in range(tensors):
            if ddp + d == 0:
                continue
            pl.semaphore_signal(
                barrier, inc=1,
                device_id=(lax.rem(dp + ddp, dps), y, lax.rem(t + d, tensors)),
                device_id_type=MESH,
            )
    pl.semaphore_signal(barrier, inc=1, device_id=(dp, oy, t), device_id_type=MESH)
    pl.semaphore_wait(barrier, dps * tensors)

    pieces = CHUNKS + groups

    def piece(i, own_in, in_slot, own_out):
        if i < CHUNKS:
            size = width // (2 * CHUNKS)
            at = pl.ds(pl.multiple_of((dp * CHUNKS + i) * size, 128), size)
            return own_in.at[:, at] if in_slot is None else own_in.at[in_slot, :, at]
        at = pl.ds(pl.multiple_of(dp * (depth // 2), 16), depth // 2)
        return own_out.at[at, pl.ds((i - CHUNKS) * 128, 128)]

    ycopies = []
    xcopies = []

    def send_y():
        i = len(ycopies)
        if i < pieces:
            ycopies.append(
                remote(
                    piece(i, pin_hbm, None, bout_hbm), piece(i, pin, y, bout_oth),
                    ysend.at[i], yrecv.at[i], (dp, oy, t),
                )
            )

    def forward():
        i = len(xcopies)
        ycopies[i].wait_recv()
        send_y()
        ref = piece(i, pin, oy, bout_oth)
        xcopies.append(remote(ref, ref, xsend.at[i], xrecv.at[i], (odp, y, t)))

    mates = []

    def project_grad(basis, first, number):
        n = len(mates)
        total = lax.dot_general(
            basis, grad[...], (((0,), (1,)), ((), ())), preferred_element_type=F32
        )
        gpart[first : first + number] = total.reshape(number, 2, nz, cols, tokens)
        part = pl.ds(first, number)
        mates.append(
            remote(
                gpart.at[part, 1 - c], gmate.at[part], msend.at[n], mrecv.at[n],
                (dp, y, mate),
            )
        )

    zcopies = []

    def scatter_grad(n, first, number):
        mates[n].wait_recv()
        part = pl.ds(first, number)
        gsend[part] = (gpart[part, c] + gmate[part]).astype(BF16)
        gown[part] = gpart[part, c, z] + gmate[part, z]
        copies = []
        for d in range(1, nz):
            oz = lax.rem(z + d, nz)
            i = n * (nz - 1) + d - 1
            copies.append(
                remote(
                    gsend.at[part, oz], grecv.at[d - 1, part], zsend.at[i], zrecv.at[i],
                    (dp, y, oz * 2 + c),
                )
            )
        zcopies.append(copies)

    def finish_grad(n, first, number):
        part = pl.ds(first, number)
        total = gown[part]
        for d in range(1, nz):
            zcopies[n][d - 1].wait_recv()
            total = total + grecv[d - 1, part].astype(F32)
        gfin[part] = total.astype(BF16)

    def project_act(half):
        at = pl.ds(pl.multiple_of(half * (width // 2), 128), width // 2)
        basis = pin[:, :, at].reshape(kk, width // 2)
        return lax.dot_general(
            act[:, at], basis, (((1,), (1,)), ((), ())), preferred_element_type=F32
        )

    def outer(slot, masked0, masked1):
        at = jnp.where(y == slot, 0, 1)
        part = gfin[slot * groups : (slot + 1) * groups].reshape(groups * cols, tokens)
        bpart[0, at] = jnp.dot(part, masked0, preferred_element_type=F32)
        bpart[1, at] = jnp.dot(part, masked1, preferred_element_type=F32)

    send_y()
    send_y()
    loads[0].wait()
    loads[1].wait()
    project_grad(bout_own[...], 0, groups)
    forward()
    loads[2].wait()
    loads[3].wait()
    forward()
    apart[...] = project_act(dp).reshape(apart.shape)
    scatter_grad(0, 0, groups)
    forward()
    for i in range(CHUNKS):
        xcopies[i].wait_recv()
    apart[...] = apart[...] + project_act(odp).reshape(apart.shape)
    a1 = []
    for d in range(1, tensors):
        ot = lax.rem(t + d, tensors)
        a1.append(
            remote(apart.at[ot], arecv.at[d - 1], a1send.at[d - 1], a1recv.at[d - 1], (dp, y, ot))
        )
    a2 = []
    for g in range(groups):
        if g + 1 < groups:
            forward()
        if g == 1:
            total = apart[t]
            for d in range(1, tensors):
                a1[d - 1].wait_recv()
                total = total + arecv[d - 1]
            afull[t] = total.astype(BF16)
            for d in range(1, tensors):
                ot = lax.rem(t + d, tensors)
                a2.append(
                    remote(
                        afull.at[t], afull.at[t], a2send.at[d - 1], a2recv.at[d - 1],
                        (dp, y, ot),
                    )
                )
        if g == groups - 1:
            finish_grad(0, 0, groups)
        xcopies[CHUNKS + g].wait_recv()
        project_grad(bout_oth[:, g * 128 : (g + 1) * 128], groups + g, 1)
        if g > 0:
            scatter_grad(g, groups + g - 1, 1)
    for copy in a2:
        copy.wait_recv()
    whole = afull[...].astype(F32).reshape(tokens, kk)
    turned = pltpu.roll(whole, kk // 2, 1)
    lane = lax.broadcasted_iota(jnp.int32, (tokens, kk), 1)
    row = lax.broadcasted_iota(jnp.int32, (tokens, kk), 0)
    low = lane < kk // 2
    mine = (row < per_seq) == low
    masked0 = jnp.where(mine, jnp.where(low, whole, turned), 0.0).astype(BF16)
    masked1 = jnp.where(mine, jnp.where(low, turned, whole), 0.0).astype(BF16)
    scatter_grad(groups, 2 * groups - 1, 1)
    outer(0, masked0, masked1)
    spad[...] = jnp.zeros_like(spad)
    for g in range(groups):
        finish_grad(1 + g, groups + g, 1)
    outer(1, masked0, masked1)
    bcopy = remote(bpart.at[oy], brecv, bsend.at[0], brecv_sem.at[0], (dp, oy, t))
    bcopy.wait_recv()
    both = (bpart[y] + brecv[...]).reshape(2 * groups * cols, kk)
    square = both * both
    spad[pl.ds(0, 2 * groups * cols), :] = square + pltpu.roll(square, kk // 2, 1)
    strans[...] = spad[...].T.reshape(strans.shape)
    place = c * nz + z
    frecv[0, place] = strans[t]
    fcopies = []
    for ddp in range(dps):
        for d in range(tensors):
            if ddp + d == 0:
                continue
            i = ddp * tensors + d - 1
            ot = lax.rem(t + d, tensors)
            fcopies.append(
                remote(
                    strans.at[ot], frecv.at[ddp, place], fsend.at[i], frecv_sem.at[i],
                    (lax.rem(dp + ddp, dps), y, ot),
                )
            )
    for copy in fcopies:
        copy.wait_recv()
    total = (frecv[0] + frecv[1]) / count
    lane = lax.broadcasted_iota(jnp.int32, total.shape[1:], 1)
    for block in range(2 * groups):
        found = jnp.zeros(total.shape[1:], F32)
        for p in range(tensors):
            shift = ((p - block) * cols) % 128
            moved = pltpu.roll(total[p], shift, 1) if shift else total[p]
            found = jnp.where(lane // cols == p, moved, found)
        out_ref[:, block * 128 : (block + 1) * 128] = found
    zall = [copy for copies in zcopies for copy in copies]
    for copy in ycopies + xcopies + mates + zall + a1 + a2 + [bcopy] + fcopies:
        copy.wait_send()


def fused(activations, gradients, basis_in, basis_out):
    dps, seqs, tensors = lax.axis_size("dp"), lax.axis_size("seq"), lax.axis_size("tensor")
    s, length, width = activations.shape
    gwidth = gradients.shape[2]
    tokens = s * length
    nz = tensors // 2
    khalf = basis_in.shape[1]
    jhalf = basis_out.shape[1]
    kk = 2 * khalf
    groups = jhalf // 128
    cols = 128 // tensors
    per = khalf // tensors
    count = s * dps * length * seqs
    dma = pltpu.SemaphoreType.DMA
    tok_own = tokens // tensors
    pieces = CHUNKS + groups
    shifts = (1 + groups) * (nz - 1)
    return pl.pallas_call(
        functools.partial(kernel, (dps, seqs, tensors, nz, groups, cols, count)),
        out_shape=jax.ShapeDtypeStruct((per, 2 * jhalf), F32),
        in_specs=[pl.BlockSpec(memory_space=pltpu.HBM)] * 4,
        out_specs=pl.BlockSpec(memory_space=pltpu.VMEM),
        scratch_shapes=[
            pltpu.VMEM((tokens, width), BF16),
            pltpu.VMEM((tokens, gwidth), BF16),
            pltpu.VMEM((2, khalf, width), BF16),
            pltpu.VMEM((gwidth, jhalf), BF16),
            pltpu.VMEM((gwidth, jhalf), BF16),
            pltpu.VMEM((2 * groups, 2, nz, cols, tokens), F32),
            pltpu.VMEM((2 * groups, nz, cols, tokens), F32),
            pltpu.VMEM((2 * groups, cols, tokens), F32),
            pltpu.VMEM((2 * groups, nz, cols, tokens), BF16),
            pltpu.VMEM((nz - 1, 2 * groups, cols, tokens), BF16),
            pltpu.VMEM((2 * groups, cols, tokens), BF16),
            pltpu.VMEM((tensors, tok_own, kk), F32),
            pltpu.VMEM((tensors - 1, tok_own, kk), F32),
            pltpu.VMEM((tensors, tok_own, kk), BF16),
            pltpu.VMEM((2, 2, groups * cols, kk), F32),
            pltpu.VMEM((2, groups * cols, kk), F32),
            pltpu.VMEM((128, kk), F32),
            pltpu.VMEM((kk // per, per, 128), F32),
            pltpu.VMEM((dps, tensors, per, 128), F32),
            dma((4,)),
            dma((pieces,)), dma((pieces,)),
            dma((pieces,)), dma((pieces,)),
            dma((1 + groups,)), dma((1 + groups,)),
            dma((shifts,)), dma((shifts,)),
            dma((tensors - 1,)), dma((tensors - 1,)),
            dma((tensors - 1,)), dma((tensors - 1,)),
            dma((1,)), dma((1,)),
            dma((dps * tensors - 1,)), dma((dps * tensors - 1,)),
        ],
        compiler_params=pltpu.CompilerParams(
            collective_id=0, has_side_effects=True, vmem_limit_bytes=56 * 1024 * 1024
        ),
    )(
        activations.reshape(tokens, width),
        gradients.reshape(tokens, gwidth),
        basis_in.T,
        basis_out,
    )


def general(activations, gradients, basis_in, basis_out):
    seq_count = lax.axis_size("seq")
    tensor_count = lax.axis_size("tensor")
    replica_count = lax.axis_size("dp")
    seqs_local = activations.shape[0]
    len_local = activations.shape[1]
    width_local = activations.shape[2]
    grad_partial = jnp.einsum(
        "sci,ij->scj",
        gradients,
        lax.all_gather(basis_out, "seq", axis=1, tiled=True),
        preferred_element_type=jnp.float32,
    )
    projected_grad = lax.psum(grad_partial, "tensor").astype(jnp.bfloat16)
    whole_basis = lax.all_gather(basis_in, "seq", axis=1, tiled=True)
    col_total = whole_basis.shape[1]
    per_device = col_total // (seq_count * tensor_count)
    arranged = whole_basis.reshape(width_local, seq_count, tensor_count, per_device)
    group_rows = seq_count * per_device
    product = jnp.einsum(
        "isTj,qci->Tsjqc", arranged, activations, preferred_element_type=jnp.float32
    )
    flat_act = lax.psum_scatter(
        product.reshape(group_rows * lax.axis_size("tensor"), seqs_local * len_local),
        "tensor",
        scatter_dimension=0,
        tiled=True,
    ).astype(jnp.bfloat16)
    projected_act = flat_act.reshape(flat_act.shape[0], seqs_local, len_local)
    partial_blocks = jnp.einsum(
        "rqc,qcj->qrj", projected_act, projected_grad, preferred_element_type=jnp.float32
    )
    blocks = lax.psum_scatter(partial_blocks, "seq", scatter_dimension=1, tiled=True)
    squared = jnp.sum(blocks * blocks, axis=0)
    summed = lax.psum(squared, "dp")
    return summed / (seqs_local * replica_count * len_local * seq_count)


def body(activations, gradients, basis_in, basis_out):
    dps, seqs, tensors = lax.axis_size("dp"), lax.axis_size("seq"), lax.axis_size("tensor")
    s, length, width = activations.shape
    tokens = s * length
    khalf, jhalf = basis_in.shape[1], basis_out.shape[1]
    fits = (
        dps == 2 and seqs == 2 and s == 2 and tensors == 8
        and khalf == 64 and khalf % (8 * tensors) == 0
        and tokens % (16 * tensors) == 0 and tokens % 128 == 0
        and jhalf % 128 == 0 and 2 * jhalf // tensors <= 128 and jhalf >= 256
        and width % (256 * CHUNKS) == 0 and gradients.shape[2] % 32 == 0
        and tokens * width * 2 <= 8 * 1024 * 1024
    )
    return (fused if fits else general)(activations, gradients, basis_in, basis_out)


def solution(mesh):
    return jax.shard_map(
        body,
        mesh=mesh,
        in_specs=(
            P("dp", "seq", "tensor"),
            P("dp", "seq", "tensor"),
            P("tensor", "seq"),
            P("tensor", "seq"),
        ),
        out_specs=P(("seq", "tensor"), None),
        check_vma=False,
    )
```

time: 53.6 us -> 42.6 us (0.79)
  local copies, waits for them, and re-layouts: 9.15 us -> 1.35 us
  Pallas kernels: 42.7 us -> 41.1 us
  other arithmetic: 1.41 us -> 0 us
    unnamed x10 -> x1, local copies, waits for them, and re-layouts: 5.57 us -> 1.35 us
    slice x1 -> x0, local copies, waits for them, and re-layouts: 2.01 us -> none  [fused(): basis_in[:width // 2]]
    pallas_call x1, Pallas kernels: 42.7 us -> 41.1 us  [fused(): pl.pallas_call(functools.partial(kernel, (dps, seqs, tensors, nz, groups,...]
    reshape x2 -> x0, local copies, waits for them, and re-layouts: 1.55 us -> none  [the longest x1 0.85 us: fused(): kept = out[:, :, :2 * cols].reshape(tensors, per, 2, cols)]
    concatenate x1 -> x0, other arithmetic: 1.41 us -> none  [fused(): jnp.concatenate([basis_in[:width // 2], basis_in[width // 2:]], axis=1)]
where the time goes in v2:
time: 42.6 us; the launch traced here: 42.4 us
  Pallas kernels  41.1 us (96%)
  local copies, waits for them, and re-layouts  1.35 us (3%)
    pallas_call x1, Pallas kernels, fused(): pl.pallas_call(functools.partial(kernel, (dps, seqs, tensors, nz, groups,...  41.1 us
    unnamed x1, local copies, waits for them, and re-layouts  1.35 us

profile of v2, /device:TPU:0, one launch (start us, length us, event | category | flops | bytes accessed | tf_op | source)
XLA Modules:
  0.0 42.4 jit_solution(4428963818128934195)
XLA Ops:
  0.0 41.1 %shard_map.46 = f32[8,768]{1,0:T(8,128)} custom-call(bf16[384,3584]{1,0:T(8,128)(2,1)} %bitcast.3, bf16[384,1024]{1,0:T(8,128)(2,1)} %bitcast.4, bf16[64,3584]{1,0:T(8,128)(2,1)} %bitcast.5, bf16[1024,384]{1,0:T(8,128)(2,1)} %bout_hbm.1), custom_call_target="tpu_custom_call" | custom-call | tf_op jit(solution)/shard_map/pallas_call | solution.py:270
  41.1 1.3 %copy.6 = f32[8,768]{1,0:T(8,128)} copy(f32[8,768]{1,0:T(8,128)} %shard_map.46) | data formatting | bytes 49152

commit v3 on v2

--- a/solution.py
+++ b/solution.py
@@ -11,6 +11,8 @@
 F32 = jnp.float32
 BF16 = jnp.bfloat16
 CHUNKS = 2
+SPLIT = 1
+DEPTH = 8
 
 
 def kernel(
@@ -66,15 +68,17 @@
     pl.semaphore_signal(barrier, inc=1, device_id=(dp, oy, t), device_id_type=MESH)
     pl.semaphore_wait(barrier, dps * tensors)
 
-    pieces = CHUNKS + groups
+    pieces = CHUNKS + SPLIT * groups
 
     def piece(i, own_in, in_slot, own_out):
         if i < CHUNKS:
             size = width // (2 * CHUNKS)
             at = pl.ds(pl.multiple_of((dp * CHUNKS + i) * size, 128), size)
             return own_in.at[:, at] if in_slot is None else own_in.at[in_slot, :, at]
-        at = pl.ds(pl.multiple_of(dp * (depth // 2), 16), depth // 2)
-        return own_out.at[at, pl.ds((i - CHUNKS) * 128, 128)]
+        g, k = divmod(i - CHUNKS, SPLIT)
+        size = depth // (2 * SPLIT)
+        at = pl.ds(pl.multiple_of((dp * SPLIT + k) * size, 16), size)
+        return own_out.at[at, pl.ds(g * 128, 128)]
 
     ycopies = []
     xcopies = []
@@ -152,18 +156,19 @@
         bpart[0, at] = jnp.dot(part, masked0, preferred_element_type=F32)
         bpart[1, at] = jnp.dot(part, masked1, preferred_element_type=F32)
 
-    send_y()
-    send_y()
+    for _ in range(DEPTH):
+        send_y()
     loads[0].wait()
     loads[1].wait()
     project_grad(bout_own[...], 0, groups)
-    forward()
     loads[2].wait()
     loads[3].wait()
-    forward()
+    for _ in range(CHUNKS):
+        forward()
     apart[...] = project_act(dp).reshape(apart.shape)
     scatter_grad(0, 0, groups)
-    forward()
+    for _ in range(SPLIT):
+        forward()
     for i in range(CHUNKS):
         xcopies[i].wait_recv()
     apart[...] = apart[...] + project_act(odp).reshape(apart.shape)
@@ -176,7 +181,8 @@
     a2 = []
     for g in range(groups):
         if g + 1 < groups:
-            forward()
+            for _ in range(SPLIT):
+                forward()
         if g == 1:
             total = apart[t]
             for d in range(1, tensors):
@@ -193,7 +199,8 @@
                 )
         if g == groups - 1:
             finish_grad(0, 0, groups)
-        xcopies[CHUNKS + g].wait_recv()
+        for k in range(SPLIT):
+            xcopies[CHUNKS + g * SPLIT + k].wait_recv()
         project_grad(bout_oth[:, g * 128 : (g + 1) * 128], groups + g, 1)
         if g > 0:
             scatter_grad(g, groups + g - 1, 1)
@@ -209,12 +216,21 @@
     masked1 = jnp.where(mine, jnp.where(low, turned, whole), 0.0).astype(BF16)
     scatter_grad(groups, 2 * groups - 1, 1)
     outer(0, masked0, masked1)
+    bcopies = [
+        remote(bpart.at[oy, y], brecv.at[y], bsend.at[0], brecv_sem.at[0], (dp, oy, t))
+    ]
     spad[...] = jnp.zeros_like(spad)
     for g in range(groups):
         finish_grad(1 + g, groups + g, 1)
     outer(1, masked0, masked1)
-    bcopy = remote(bpart.at[oy], brecv, bsend.at[0], brecv_sem.at[0], (dp, oy, t))
-    bcopy.wait_recv()
+    bcopies.append(
+        remote(bpart.at[oy, oy], brecv.at[oy], bsend.at[1], brecv_sem.at[1], (dp, oy, t))
+    )
+    zall = [copy for copies in zcopies for copy in copies]
+    for copy in ycopies + xcopies + mates + zall + a1 + a2:
+        copy.wait_send()
+    for copy in bcopies:
+        copy.wait_recv()
     both = (bpart[y] + brecv[...]).reshape(2 * groups * cols, kk)
     square = both * both
     spad[pl.ds(0, 2 * groups * cols), :] = square + pltpu.roll(square, kk // 2, 1)
@@ -236,7 +252,7 @@
             )
     for copy in fcopies:
         copy.wait_recv()
-    total = (frecv[0] + frecv[1]) / count
+    total = frecv[0] + frecv[1]
     lane = lax.broadcasted_iota(jnp.int32, total.shape[1:], 1)
     for block in range(2 * groups):
         found = jnp.zeros(total.shape[1:], F32)
@@ -245,8 +261,7 @@
             moved = pltpu.roll(total[p], shift, 1) if shift else total[p]
             found = jnp.where(lane // cols == p, moved, found)
         out_ref[:, block * 128 : (block + 1) * 128] = found
-    zall = [copy for copies in zcopies for copy in copies]
-    for copy in ycopies + xcopies + mates + zall + a1 + a2 + [bcopy] + fcopies:
+    for copy in bcopies + fcopies:
         copy.wait_send()
 
 
@@ -265,9 +280,9 @@
     count = s * dps * length * seqs
     dma = pltpu.SemaphoreType.DMA
     tok_own = tokens // tensors
-    pieces = CHUNKS + groups
+    pieces = CHUNKS + SPLIT * groups
     shifts = (1 + groups) * (nz - 1)
-    return pl.pallas_call(
+    total = pl.pallas_call(
         functools.partial(kernel, (dps, seqs, tensors, nz, groups, cols, count)),
         out_shape=jax.ShapeDtypeStruct((per, 2 * jhalf), F32),
         in_specs=[pl.BlockSpec(memory_space=pltpu.HBM)] * 4,
@@ -299,7 +314,7 @@
             dma((shifts,)), dma((shifts,)),
             dma((tensors - 1,)), dma((tensors - 1,)),
             dma((tensors - 1,)), dma((tensors - 1,)),
-            dma((1,)), dma((1,)),
+            dma((2,)), dma((2,)),
             dma((dps * tensors - 1,)), dma((dps * tensors - 1,)),
         ],
         compiler_params=pltpu.CompilerParams(
@@ -311,6 +326,7 @@
         basis_in.T,
         basis_out,
     )
+    return total / count
 
 
 def general(activations, gradients, basis_in, basis_out):
@@ -361,7 +377,7 @@
         and khalf == 64 and khalf % (8 * tensors) == 0
         and tokens % (16 * tensors) == 0 and tokens % 128 == 0
         and jhalf % 128 == 0 and 2 * jhalf // tensors <= 128 and jhalf >= 256
-        and width % (256 * CHUNKS) == 0 and gradients.shape[2] % 32 == 0
+        and width % (256 * CHUNKS) == 0 and gradients.shape[2] % (32 * SPLIT) == 0
         and tokens * width * 2 <= 8 * 1024 * 1024
     )
     return (fused if fits else general)(activations, gradients, basis_in, basis_out)

time: 42.6 us -> 41.8 us (0.981)
  other arithmetic: 0 us -> 1.35 us
  local copies, waits for them, and re-layouts: 1.35 us -> 0 us
  Pallas kernels: 41.1 us -> 40.2 us
    div x0 -> x1, other arithmetic: none -> 1.35 us  [fused(): return total / count]
    unnamed x1 -> x0, local copies, waits for them, and re-layouts: 1.35 us -> none
    pallas_call x1, Pallas kernels: 41.1 us -> 40.2 us  [fused(): pl.pallas_call(functools.partial(kernel, (dps, seqs, tensors, nz, groups,...]
where the time goes in v3:
time: 41.8 us; the launch traced here: 41.6 us
  Pallas kernels  40.2 us (96%)
  other arithmetic  1.35 us (3%)
    pallas_call x1, Pallas kernels, fused(): pl.pallas_call(functools.partial(kernel, (dps, seqs, tensors, nz, groups,...  40.2 us
    div x1, other arithmetic, fused(): return total / count  1.35 us

profile of v3, /device:TPU:0, one launch (start us, length us, event | category | flops | bytes accessed | tf_op | source)
XLA Modules:
  0.0 41.6 jit_solution(17833842325307796109)
XLA Ops:
  0.0 40.2 %shard_map.46 = f32[8,768]{1,0:T(8,128)} custom-call(bf16[384,3584]{1,0:T(8,128)(2,1)} %bitcast.3, bf16[384,1024]{1,0:T(8,128)(2,1)} %bitcast.4, bf16[64,3584]{1,0:T(8,128)(2,1)} %bitcast.5, bf16[1024,384]{1,0:T(8,128)(2,1)} %bout_hbm.1), custom_call_target="tpu_custom_call" | custom-call | tf_op jit(solution)/shard_map/pallas_call | solution.py:285
  40.2 1.3 %broadcast_multiply_fusion = f32[8,768]{1,0:T(8,128)} fusion(f32[8,768]{1,0:T(8,128)} %shard_map.46), kind=kLoop, calls=%fused_computation | loop fusion | flops 6144 | bytes 49152 | tf_op jit(solution)/shard_map/div | solution.py:329
